TPU v7x, 512 devices: a whole 4x4x16 slice. The times are simulated.
512 devices in a mesh: chaos: 64 (over y, x, z_hi, core), space: 8 (over z_lo).
Axes of the slice: x: 4, y: 4, z: 16 (z_hi: 2, z_lo: 8; z = z_hi * 8 + z_lo), core: 2. Of those that a mesh axis runs over, the one named last changes fastest.
Arguments:
- panels: bfloat16 [256, 131072], P('chaos', 'space'), may hold values from -6 to 6
- tiles: bfloat16 [20, 8, 128, 3, 128, 128], P(None, 'space', 'chaos'), may hold values from -0.3125 to 0.3125
- coupling: bfloat16 [256, 20, 256], P('chaos'), may hold values from -0.125 to 0.125
- pattern: int32 [20, 4, 4], replicated, may hold values 0 or 1
- colidx: int32 [8, 128, 3], P('space', 'chaos'), may hold values from -2 to 1025, as said below
Outputs:
- applied: bfloat16 [256, 131072], P('chaos', 'space')
Inputs may be any that keep to these rules, and one draw needn't show every extreme that they name: `colidx`: row block r names 3 distinct tile columns: r itself and 2 of r - 2, r - 1, r + 1, r + 2; columns outside 0 .. 1023 stand for blocks of zeros.
All inputs are finite; a program needn't handle non-finite values.
Results may differ from a plain program's by a relative error of at most 0.005.
Values may be sent and summed in bfloat16 or wider, within the bound.
A program may use at most 64 MiB of HBM per device.

v0:
```python
import jax
import jax.numpy as jnp
from jax import lax
from jax.sharding import PartitionSpec as P

M = 20
TILE = 128
CBLK = 64


def extended(cells, sides, width):
    for axis, dim in sides:
        count = lax.axis_size(axis)
        ends = count - 1
        head = lax.slice_in_dim(cells, 0, width, axis=dim)
        tail = lax.slice_in_dim(cells, cells.shape[dim] - width, cells.shape[dim], axis=dim)
        cells = jnp.concatenate(
            [
                lax.ppermute(tail, axis, [(i, (i + 1) % count) for i in range(ends)]),
                cells,
                lax.ppermute(head, axis, [((i + 1) % count, i) for i in range(ends)]),
            ],
            axis=dim,
        )
    return cells


def coupled_terms(tile_rows, window, window_cols, coeff_piece):
    count = window.shape[0]
    width = coeff_piece.shape[2]
    row_count = tile_rows.shape[1]
    gathered = jnp.take(window, window_cols, axis=1)
    groups = M // 5
    tile_groups = tile_rows.reshape((groups, 5) + tile_rows.shape[1:])
    coeff_groups = jnp.transpose(coeff_piece.reshape(count, groups, 5, width), (1, 0, 2, 3))

    def add_group(running_sum, members):
        tile_group, coeff_group = members
        partial_z = jnp.einsum(
            "mrqtc,arqc->mrta", tile_group, gathered, preferred_element_type=jnp.float32
        )
        partial_z = partial_z.astype(jnp.bfloat16)
        update = jnp.einsum(
            "mrta,amb->brt", partial_z, coeff_group, preferred_element_type=jnp.float32
        )
        return (running_sum + update, None)

    start_sum = jnp.zeros((width, row_count, TILE), jnp.float32)
    running_sum, ignored = lax.scan(add_group, start_sum, (tile_groups, coeff_groups))
    return running_sum


def shards(panels, tiles, coupling, pattern, colidx):
    chaos_count = lax.axis_size("chaos")
    chaos_rank = lax.axis_index("chaos")
    space_rank = lax.axis_index("space")
    local_coeffs = panels.shape[0]
    slab_rows = panels.shape[1]
    slab_blocks = slab_rows // TILE
    own_blocks = slab_blocks // chaos_count
    total_coeffs = local_coeffs * chaos_count
    alpha_ids = chaos_rank * local_coeffs + jnp.arange(local_coeffs, dtype=jnp.int32)
    pattern_rows = jnp.take(pattern, alpha_ids // CBLK, axis=1)
    pattern_wide = jnp.repeat(pattern_rows, CBLK, axis=2)
    masked = coupling * jnp.transpose(pattern_wide, (1, 0, 2)).astype(jnp.bfloat16)
    padded = extended(panels, (("space", 1),), 2 * TILE)
    padded_blocks = padded.reshape(local_coeffs, slab_blocks + 4, TILE)
    tile_rows = tiles[:, 0]
    first_own = chaos_rank * own_blocks
    window_cols = colidx[0] - space_rank * slab_blocks - first_own + 2
    block_piece = lax.all_gather(padded_blocks, "chaos", axis=0, tiled=True)
    coeff_piece = lax.all_gather(masked, "chaos", axis=0, tiled=True)
    window = lax.dynamic_slice_in_dim(block_piece, first_own, own_blocks + 4, 1)
    summed = coupled_terms(tile_rows, window, window_cols, coeff_piece)
    flat_rows = summed.reshape(total_coeffs, own_blocks * TILE).astype(jnp.bfloat16)
    return lax.all_to_all(flat_rows, "chaos", split_axis=0, concat_axis=1, tiled=True)


def solution(mesh):
    in_specs = (
        P("chaos", "space"),
        P(None, "space", "chaos", None, None, None),
        P("chaos", None, None),
        P(),
        P("space", "chaos", None),
    )
    out_specs = P("chaos", "space")
    return jax.shard_map(shards, mesh=mesh, in_specs=in_specs, out_specs=out_specs, check_vma=False)
```

profile of v0, /device:TPU:1, one launch (start us, length us, event | category | flops | bytes accessed | tf_op | source)
XLA Modules:
  0.0 356.5 jit_solution(15543828634526371384)
XLA Ops:
  6.6 0.6 copy-done
  8.3 0.8 bitcast_multiply_fusion
  9.1 0.6 copy.19
  9.8 0.7 fusion.12
  10.5 4.4 %collective-permute-start = (bf16[4,256]{1,0:T(4,128)(2,1)S(1)}, bf16[4,256]{1,0:T(4,128)(2,1)S(1)}, u32[]{:S(2)}, u32[]{:S(2)}) collective-permute-start(bf16[4,256]{1,0:T(4,128)(2,1)S(1)} %get-tuple-element.71), channel_id=1, source_target_pairs={{0,1},{1,2},{2,3},{3,4},{4,5},{5,6},{6,7},{8,9},{9,10},{10,11},{11... | collective-permute-start | bytes 6152 | tf_op jit(solution)/shard_map/ppermute | solution.py:19
  14.9 1.3 collective-permute-start.1
  16.2 3.2 collective-permute-done.1
  19.4 1.0 pad_maximum_fusion
  20.4 0.7 reshape.128
  21.1 0.7 compare_select_fusion
  21.9 0.7 compare_and_fusion
  22.6 117.1 %all-gather.3.cloned.1.call-done = bf16[256,20,256]{2,1,0:T(8,128)(2,1)} async-done(((bf16[4,20,256]{2,1,0:T(8,128)(2,1)}), bf16[256,20,256]{2,1,0:T(8,128)(2,1)}) %all-gather.3.cloned.1.call-update) | async-done | bytes 2621456 | tf_op jit(solution)/shard_map/all_gather | solution.py:72
  139.7 3.7 %copy.28 = bf16[256,20,256]{0,2,1:T(8,128)(2,1)S(1)} copy(bf16[256,20,256]{2,1,0:T(8,128)(2,1)} %all-gather.3.cloned.1.call-done) | data formatting | bytes 5242880 | tf_op jit(solution)/shard_map/transpose | solution.py:35
  143.4 168.1 %all-gather.5.cloned.1.call-done = bf16[256,132,128]{2,1,0:T(8,128)(2,1)} async-done(((bf16[4,132,128]{2,1,0:T(8,128)(2,1)}), bf16[256,132,128]{2,1,0:T(8,128)(2,1)}) %all-gather.5.cloned.1.call-update) | async-done | bytes 8650768 | tf_op jit(solution)/shard_map/all_gather | solution.py:71
  311.5 1.4 constant_dynamic-slice_fusion.1
  313.0 0.6 gather_fusion.1
  313.8 11.9 %while.11 = (s32[]{:T(128)}, f32[256,2,128]{2,0,1:T(8,128)}, bf16[4,256,5,256]{1,3,2,0:T(8,128)(2,1)S(1)}, bf16[4,5,2,3,128,128]{5,4,3,2,1,0:T(8,128)(2,1)}, bf1...) while((s32[]{:T(128)}, f32[256,2,128]{2,0,1:T(8,128)}, ...), condition=%wide.region_1.2_spmd.clone, body=%wide.region_0.1_spmd.clone.sunk | while | flops 419889152 | bytes 2557015 | solution.py:49
  313.8 2.9 fusion.18
  316.7 3.0 fusion.18
  319.7 3.0 fusion.18
  322.6 3.0 fusion.18
  325.6 1.0 convert_element_type.26
  326.8 22.2 %all_to_all.16 = bf16[64,4,256]{2,1,0:T(4,128)(2,1)S(1)} all-to-all(bf16[64,4,256]{2,1,0:T(4,128)(2,1)S(1)} %convert_element_type.27), channel_id=1, replica_groups=mesh['chaos'=64,'space'=8] {'chaos'}, dimensions={0} | all-to-all | bytes 262144 | tf_op jit(solution)/shard_map/all_to_all | solution.py:76
  349.0 0.7 copy.43
  (21 shorter events, 1.7 us)
Async XLA Ops:
  6.5 0.7 copy-start
  6.5 133.2 %all-gather.3.cloned.1.call-start = ((), (), s32[]{:S(2)}) async-start(), calls=%async_computation.1 | async-start | bytes 3194880 | tf_op jit(solution)/shard_map/all_gather | solution.py:72
  9.8 301.8 %all-gather.5.cloned.1.call-start = ((), (), s32[]{:S(2)}) async-start(), calls=%async_computation.2 | async-start | bytes 9052160 | tf_op jit(solution)/shard_map/all_gather | solution.py:71
  10.5 5.7 %collective-permute-start = (bf16[4,256]{1,0:T(4,128)(2,1)S(1)}, bf16[4,256]{1,0:T(4,128)(2,1)S(1)}, u32[]{:S(2)}, u32[]{:S(2)}) collective-permute-start(bf16[4,256]{1,0:T(4,128)(2,1)S(1)} %get-tuple-element.71), channel_id=1, source_target_pairs={{0,1},{1,2},{2,3},{3,4},{4,5},{5,6},{6,7},{8,9},{9,10},{10,11},{11... | collective-permute-start | bytes 6152 | tf_op jit(solution)/shard_map/ppermute | solution.py:19
  14.9 4.5 %collective-permute-start.1 = (bf16[4,256]{1,0:T(4,128)(2,1)S(1)}, bf16[4,256]{1,0:T(4,128)(2,1)S(1)}, u32[]{:S(2)}, u32[]{:S(2)}) collective-permute-start(bf16[4,256]{1,0:T(4,128)(2,1)S(1)} %get-tuple-element.72), channel_id=1, source_target_pairs={{1,0},{2,1},{3,2},{4,3},{5,4},{6,5},{7,6},{9,8},{10,9},{11,10},{12... | collective-permute-start | bytes 6152 | tf_op jit(solution)/shard_map/ppermute | solution.py:21
Sparse Core Ops, SparseCore 0:
  11.7 127.9 all-gather.2
  144.1 167.4 all-gather.4
where the time goes:
time: 357 us
  waiting for transfers between devices  288 us (81%)
  blocking collectives  22.2 us (6%)
  between operations  13.5 us (4%)
  matrix products  11.8 us (3%)
  local copies, waits for them, and re-layouts  10.4 us (3%)
  starting transfers between devices  5.69 us (2%)
  other arithmetic  4.36 us (1%)
    all_gather x1, waiting for transfers between devices, shards(): block_piece = lax.all_gather(padded_blocks, 'chaos', axis=0, tiled=True)  168 us
    all_gather x1, waiting for transfers between devices, shards(): coeff_piece = lax.all_gather(masked, 'chaos', axis=0, tiled=True)  117 us
    all_to_all x1, blocking collectives, shards(): lax.all_to_all(flat_rows, 'chaos', split_axis=0, concat_axis=1, tiled=True)  22.2 us
    dot_general x4, matrix products, add_group(): jnp.einsum('mrta,amb->brt', partial_z, coeff_group, preferred_element_typ...  11.8 us
  transfers between devices with their start and end apart: 4, of which 3 were waited for; matrix products, arithmetic and copies ran while one was open for 2% of the time, Pallas kernels for 0%

commit v1 on v0

v1 whole, which is shorter than its diff:
```python
import jax
import jax.numpy as jnp
from jax import lax
from jax.experimental import pallas as pl
from jax.experimental.pallas import tpu as pltpu
from jax.sharding import PartitionSpec as P

M = 20
TILE = 128
CBLK = 64
BF = jnp.bfloat16
F32 = jnp.float32
UNITS = 33
SPLIT = 48
ORDER = (2, 1, 3, 0)


def perm(rows, source_of):
    out_row = lax.broadcasted_iota(jnp.int32, (rows, rows), 0)
    in_row = lax.broadcasted_iota(jnp.int32, (rows, rows), 1)
    return jnp.where(in_row == source_of(out_row), 1.0, 0.0).astype(BF)


def matmul(a, b):
    return lax.dot_general(a, b, (((1,), (0,)), ((), ())), preferred_element_type=F32)


def matmul_nt(a, b):
    return lax.dot_general(a, b, (((1,), (1,)), ((), ())), preferred_element_type=F32)


def kernel(cols, u, chunk, tiles, out,
           tv, uin, ufix, vbuf, xraw, xw, eraw, ew, zbuf, acc, ob, oin, fb,
           s_t, s_v, r_v, s_e, r_e, s_u, r_u, s_a, r_a, s_b, r_b, s_d, r_d, s_x, r_x, s_o, r_o, s_p, r_p):
    rank = lax.axis_index("chaos")
    s = lax.axis_index("space")
    c = rank % 2
    h = (rank // 2) % 2
    yx = rank // 4
    y = yx // 4
    x = yx % 4

    def remote(src, dst, send, recv, chaos, space=None):
        return pltpu.make_async_remote_copy(
            src_ref=src, dst_ref=dst, send_sem=send, recv_sem=recv,
            device_id={"chaos": chaos, "space": s if space is None else space},
            device_id_type=pl.DeviceIdType.MESH)

    def wait_for(ref, sem):
        pltpu.make_async_copy(ref, ref, sem).wait()

    def in_plane(dest_yx, dest_c):
        return (dest_yx * 2 + h) * 2 + dest_c

    anti = (yx * 2 + 1 - h) * 2 + c
    mate = (yx * 2 + h) * 2 + 1 - c
    low, high = s > 0, s < 7
    flat = yx * 4 + c

    load = pltpu.make_async_copy(tiles, tv, s_t)
    load.start()

    barrier = pltpu.get_barrier_semaphore()

    def greet(chaos, space):
        pl.semaphore_signal(barrier, inc=1, device_id={"chaos": chaos, "space": space},
                            device_id_type=pl.DeviceIdType.MESH)

    greet(anti, s)

    @pl.when(high)
    def _():
        greet(flat + 2 * h, s + 1)

    @pl.when(low)
    def _():
        greet(flat + 2 * h, s - 1)

    @pl.when(low & (h == 0))
    def _():
        greet(flat + 2, s - 1)

    @pl.when(high & (h == 1))
    def _():
        greet(flat, s + 1)

    def greet_plane(d, carry):
        other = (yx * 2 + c + d) % 32
        greet(in_plane(other // 2, other % 2), s)
        return carry

    lax.fori_loop(1, 32, greet_plane, 0)
    has_halo = (low & (h == 0)) | (high & (h == 1))
    pl.semaphore_wait(barrier, 32 + low.astype(jnp.int32) + high.astype(jnp.int32) + has_halo.astype(jnp.int32))

    send_right = remote(u.at[UNITS - 1], vbuf.at[h], s_v.at[0], r_v.at[h], flat, jnp.minimum(s + 1, 7))
    send_left = remote(u.at[0], vbuf.at[1 - h], s_v.at[1], r_v.at[1 - h], flat + 2, jnp.maximum(s - 1, 0))

    @pl.when(high)
    def _():
        send_right.start()

    @pl.when(low)
    def _():
        send_left.start()

    cross_e = remote(chunk, eraw.at[c, 1, y, x], s_e, r_e, anti)
    cross_e.start()
    crossings = []
    for i, shift in enumerate(ORDER):
        start = ((y + shift) % 4) * 8 + 1 - h
        crossing = remote(u.at[pl.ds(start, 8)], uin.at[pl.ds(start, 8)], s_u.at[i], r_u.at[i], anti)
        crossing.start()
        crossings.append(crossing)

    first = pl.ds(0, SPLIT)
    second = pl.ds(SPLIT, 80 - SPLIT)

    def phase_a(src, half):
        mine = eraw.at[c, half, y, x]
        for d in (1, 2, 3):
            remote(src.at[first], mine.at[first], s_a.at[half, 0], r_a.at[half, 0],
                   in_plane(y * 4 + (x + d) % 4, c)).start()
            remote(src.at[second], mine.at[second], s_a.at[half, 1], r_a.at[half, 1],
                   in_plane(((y + d) % 4) * 4 + x, c)).start()

    def phase_b(half):
        part = eraw.at[c, half]
        wait_for(part.at[0, pl.ds(0, 3), first], r_a.at[half, 0])
        row = part.at[y, :, first]
        for d in (1, 2, 3):
            remote(row, row, s_b.at[half, 0], r_b.at[half, 0], in_plane(((y + d) % 4) * 4 + x, c)).start()
        wait_for(part.at[0, pl.ds(0, 3), second], r_a.at[half, 1])
        column = part.at[:, x, second]
        for d in (1, 2, 3):
            remote(column, column, s_b.at[half, 1], r_b.at[half, 1], in_plane(y * 4 + (x + d) % 4, c)).start()

    def phase_d(half):
        part = eraw.at[c, half]
        wait_for(part.at[pl.ds(0, 3), :, first], r_b.at[half, 0])
        wait_for(part.at[pl.ds(0, 3), :, second], r_b.at[half, 1])
        remote(part, part, s_d.at[half], r_d.at[half], mate).start()

    def finish_e(half):
        part = eraw.at[c, half]
        wait_for(part.at[0, pl.ds(0, 3), first], s_a.at[half, 0])
        wait_for(part.at[0, pl.ds(0, 3), second], s_a.at[half, 1])
        wait_for(part.at[pl.ds(0, 3), :, first], s_b.at[half, 0])
        wait_for(part.at[pl.ds(0, 3), :, second], s_b.at[half, 1])
        wait_for(part, s_d.at[half])

    phase_a(chunk, 0)
    eraw[c, 0, y, x] = chunk[...]

    hub = 15 * h
    slot = yx * 2 + c

    def serve_row(src, half, shift):
        dest_y = (y + shift) % 4

        def serve(i, carry):
            dest = dest_y * 4 + (x + i // 2) % 4
            dest_c = (c + i % 2) % 2

            @pl.when((dest != hub) & (dest * 2 + dest_c != slot))
            def _():
                remote(src.at[pl.ds(dest * 2 + h, 2)], xraw.at[half, slot], s_x.at[half], r_x.at[half],
                       in_plane(dest, dest_c)).start()

            return carry

        lax.fori_loop(0, 8, serve, 0)

    def serve_hub(src, half):
        @pl.when(has_halo)
        def _():
            wait_for(vbuf.at[half], r_v.at[half])

        @pl.when(jnp.logical_not(has_halo))
        def _():
            vbuf[half] = jnp.zeros((16, TILE), BF)

        halo = vbuf[half]
        none = jnp.zeros_like(halo)
        ufix[half, 0] = src[31 * h] + jnp.where(h == 0, halo, none)
        ufix[half, 1] = src[31 * h + 1] + jnp.where(h == 1, halo, none)
        for dest_c in (0, 1):
            @pl.when(hub * 2 + dest_c != slot)
            def _():
                remote(ufix.at[half], xraw.at[half, slot], s_x.at[half], r_x.at[half],
                       in_plane(hub, dest_c)).start()

        @pl.when(yx == hub)
        def _():
            xraw[half, slot] = ufix[half]

        @pl.when(yx != hub)
        def _():
            xraw[half, slot] = src[pl.ds(yx * 2 + h, 2)]

    for shift in ORDER:
        serve_row(u, 0, shift)
    phase_b(0)
    serve_hub(u, 0)

    cross_e.wait_recv()
    phase_a(eraw.at[c, 1, y, x], 1)
    phase_d(0)
    for i, shift in enumerate(ORDER):
        crossings[i].wait_recv()
        serve_row(uin, 1, shift)
        if i == 1:
            phase_b(1)
    serve_hub(uin, 1)

    x_perm = perm(256, lambda o: ((o % 32) // 4) * 32 + (o // 32) * 4 + o % 4)
    e_perm = perm(256, lambda o: ((o % 8) // 4) * 128 + ((o % 64) // 8) * 16 + (o // 64) * 4 + o % 4)

    def ready_x(half):
        wait_for(xraw.at[half, pl.ds(0, 31)], r_x.at[half])
        for g in range(4):
            part = matmul(x_perm, xraw[half, pl.ds(g * 8, 8)].reshape(256, TILE)).astype(BF)
            for block in range(8):
                xw[half, block, pl.ds(g * 32, 32)] = part[block * 32:(block + 1) * 32]

    def ready_e(half):
        wait_for(eraw.at[1 - c, half], r_d.at[half])

        def group(kg, carry):
            rows = pl.ds(pl.multiple_of(kg * 16, 16), 16)
            for g in range(2):
                raw = eraw[:, half, pl.ds(g * 2, 2), :, rows]
                part = matmul(e_perm, raw.reshape(256, 256)).astype(BF)
                for k in range(4):
                    ew[half, kg * 4 + k, pl.ds(g * 64, 64)] = part[k * 64:(k + 1) * 64]
            return carry

        lax.fori_loop(0, 5, group, 0)

    def stage_one(half):
        for r in range(2):
            picked = [xw[half, cols[r, q]] for q in range(3)]
            pair = jnp.concatenate(picked[:2], axis=1)

            def some(kg, carry):
                part = tv[pl.ds(kg * 4, 4), r]
                left = jnp.concatenate([part[:, 0], part[:, 1]], axis=2).reshape(512, 256)
                z = matmul_nt(left, pair) + matmul_nt(part[:, 2].reshape(512, TILE), picked[2])
                z = z.astype(BF)
                for k in range(4):
                    zbuf[kg * 2 + k // 2, pl.ds(r * TILE, TILE), pl.ds((k % 2) * TILE, TILE)] = z[k * TILE:(k + 1) * TILE]
                return carry

            lax.fori_loop(0, 5, some, 0)

    def stage_two(half):
        def pair_of(kk, total):
            return total + matmul(zbuf[kk], ew[half, pl.ds(kk * 2, 2)].reshape(256, 256))

        return lax.fori_loop(0, 10, pair_of, jnp.zeros((256, 256), F32))

    load.wait()
    ready_x(0)
    stage_one(0)
    phase_d(1)
    ready_e(0)
    acc[...] = stage_two(0)
    ready_e(1)
    ready_x(1)
    stage_one(1)
    total = (acc[...] + stage_two(1)).astype(BF)

    o_perm = perm(256, lambda o: ((o % 64) // 4) * 16 + (o // 128) * 8 + ((o % 128) // 64) * 4 + o % 4)
    ob[...] = matmul_nt(o_perm, total).astype(BF)
    cross_o = remote(ob.at[pl.ds(pl.multiple_of((1 - h) * 128, 128), 128)], oin, s_o, r_o, anti)
    cross_o.start()
    mine = ob[pl.ds(pl.multiple_of(h * 128, 128), 128)]
    f_perm = perm(256, lambda o: ((o % 16) // 4) * 64 + (o // 16) * 4 + o % 4)
    cross_o.wait_recv()
    theirs = oin[...]
    lower = jnp.where(h == 0, mine, theirs)
    upper = jnp.where(h == 0, theirs, mine)
    for dest_c in range(2):
        rows = slice(dest_c * 64, dest_c * 64 + 64)
        stack = jnp.concatenate([lower[rows, :TILE], lower[rows, TILE:], upper[rows, :TILE], upper[rows, TILE:]], axis=0)
        fb[dest_c] = matmul(f_perm, stack).astype(BF).reshape(16, 16, TILE)

    def give(d, carry):
        other = (slot + d) % 32
        remote(fb.at[other % 2, other // 2], out.at[slot], s_p, r_p, in_plane(other // 2, other % 2)).start()
        return carry

    lax.fori_loop(1, 32, give, 0)
    out[slot] = fb[c, yx]

    @pl.when(high)
    def _():
        send_right.wait_send()

    @pl.when(low)
    def _():
        send_left.wait_send()

    cross_e.wait_send()
    for crossing in crossings:
        crossing.wait_send()
    for half in (0, 1):
        finish_e(half)
        wait_for(xraw.at[half, pl.ds(0, 31)], s_x.at[half])
    cross_o.wait_send()
    wait_for(out.at[pl.ds(0, 31)], s_p)
    wait_for(out.at[pl.ds(0, 31)], r_p)


def shards(panels, tiles, coupling, pattern, colidx):
    rank = lax.axis_index("chaos")
    space = lax.axis_index("space")
    cells = jnp.transpose(panels.reshape(4, 128, TILE), (1, 0, 2)).reshape(512, TILE)
    units = jnp.pad(cells, ((8, 8), (0, 0))).reshape(UNITS, 16, TILE)
    own_pattern = lax.dynamic_index_in_dim(pattern, rank // 16, 1, keepdims=False).astype(BF)
    mask = jnp.broadcast_to(own_pattern[:, None, :, None], (M, 4, 4, CBLK)).reshape(M, 4, 256)
    chunk = (jnp.transpose(coupling, (1, 0, 2)) * mask).reshape(80, 256)
    cols = colidx[0] - (space * 128 + (rank // 2) * 4) + 2
    vmem = pl.BlockSpec(memory_space=pltpu.VMEM)
    dma = pltpu.SemaphoreType.DMA
    result = pl.pallas_call(
        kernel,
        name="galerkin",
        out_shape=jax.ShapeDtypeStruct((32, 16, TILE), BF),
        in_specs=[pl.BlockSpec(memory_space=pltpu.SMEM), vmem, vmem, pl.BlockSpec(memory_space=pl.ANY)],
        out_specs=vmem,
        scratch_shapes=[
            pltpu.VMEM((M, 2, 3, TILE, TILE), BF),
            pltpu.VMEM((UNITS, 16, TILE), BF),
            pltpu.VMEM((2, 2, 16, TILE), BF),
            pltpu.VMEM((2, 16, TILE), BF),
            pltpu.VMEM((2, 32, 2, 16, TILE), BF),
            pltpu.VMEM((2, 8, TILE, TILE), BF),
            pltpu.VMEM((2, 2, 4, 4, 80, 256), BF),
            pltpu.VMEM((2, M, TILE, 256), BF),
            pltpu.VMEM((10, 256, 256), BF),
            pltpu.VMEM((256, 256), F32),
            pltpu.VMEM((256, 256), BF),
            pltpu.VMEM((TILE, 256), BF),
            pltpu.VMEM((2, 16, 16, TILE), BF),
            dma, dma((2,)), dma((2,)), dma, dma, dma((4,)), dma((4,)),
            dma((2, 2)), dma((2, 2)), dma((2, 2)), dma((2, 2)), dma((2,)), dma((2,)), dma((2,)), dma((2,)),
            dma, dma, dma, dma,
        ],
        compiler_params=pltpu.CompilerParams(collective_id=0, has_side_effects=True, vmem_limit_bytes=40 << 20),
        cost_estimate=pl.CostEstimate(flops=2_000_000_000, bytes_accessed=8_000_000, transcendentals=0),
    )(cols, units, chunk, tiles.reshape(M, 2, 3, TILE, TILE))
    parts = result.reshape(16, 2, 2, 2, 4, TILE)
    return jnp.transpose(parts, (4, 0, 2, 1, 3, 5)).reshape(4, 128 * TILE)


def solution(mesh):
    in_specs = (
        P("chaos", "space"),
        P(None, "space", "chaos", None, None, None),
        P("chaos", None, None),
        P(),
        P("space", "chaos", None),
    )
    return jax.shard_map(shards, mesh=mesh, in_specs=in_specs, out_specs=P("chaos", "space"), check_vma=False)
```

time: 357 us -> 73.9 us (0.21)
  waiting for transfers between devices: 288 us -> 0 us
  Pallas kernels: 0 us -> 66.4 us
  blocking collectives: 22.2 us -> 0 us
  between operations: 13.5 us -> 0.06 us
  matrix products: 11.8 us -> 0 us
  local copies, waits for them, and re-layouts: 10.4 us -> 4.26 us
  starting transfers between devices: 5.69 us -> 0 us
    all_gather x2 -> x0, waiting for transfers between devices: 285 us -> none  [the longest x1 168 us: shards(): block_piece = lax.all_gather(padded_blocks, 'chaos', axis=0, tiled=True)]
    pallas_call x0 -> x1, Pallas kernels: none -> 66.4 us  [shards(): pl.pallas_call(kernel, name='galerkin', out_shape=jax.ShapeDtypeStruct((3...]
    all_to_all x1 -> x0, blocking collectives: 22.2 us -> none  [shards(): lax.all_to_all(flat_rows, 'chaos', split_axis=0, concat_axis=1, tiled=True)]
    dot_general x4 -> x0, matrix products: 11.8 us -> none  [add_group(): jnp.einsum('mrta,amb->brt', partial_z, coeff_group, preferred_element_typ...]
    ppermute x2 -> x0, starting transfers between devices: 5.65 us -> none  [the longest x1 4.36 us: extended(): lax.ppermute(tail, axis, [(i, (i + 1) % count) for i in range(ends)])]
  transfers between devices with their start and end apart: 4 -> 0, of which waited for: 3 -> 0; matrix products, arithmetic and copies ran while one was open for 2% -> 0% of each run, Pallas kernels for 0% -> 0%
where the time goes in v1:
time: 73.9 us; the launch traced here: 72.9 us
  Pallas kernels  66.4 us (90%)
  local copies, waits for them, and re-layouts  4.26 us (6%)
  other arithmetic  2.18 us (3%)
    pallas_call x1, Pallas kernels, shards(): pl.pallas_call(kernel, name='galerkin', out_shape=jax.ShapeDtypeStruct((3...  66.4 us
    unnamed x3, local copies, waits for them, and re-layouts  3.03 us

profile of v1, /device:TPU:1, one launch (start us, length us, event | category | flops | bytes accessed | tf_op | source)
XLA Modules:
  0.0 72.9 jit_solution(13093164578202952867)
XLA Ops:
  0.0 0.7 fusion
  0.7 0.7 add_bitcast_fusion.cols
  1.4 0.1 copy.7
  1.5 0.1 broadcast_in_dim.10
  1.6 0.1 broadcast_in_dim.11
  1.7 0.8 %multiply_bitcast_fusion = bf16[20,4,256]{2,1,0:T(4,128)(2,1)S(1)} fusion(bf16[4,20,256]{2,0,1:T(4,128)(2,1)} %param.7, bf16[20,256]{1,0:T(8,128)(2,1)S(1)} %broadcast_in_dim.11), kind=kLoop, calls=%fused_computation.1 | loop fusion | flops 20480 | bytes 92160 | tf_op jit(solution)/shard_map/mul | solution.py:322
  2.5 0.9 %copy.11 = bf16[1,4,128,128]{3,2,1,0:T(8,128)(2,1)S(1)} copy(bf16[1,4,128,128]{3,1,2,0:T(4,128)(2,1)} %bitcast.24) | data formatting | bytes 262144
  3.4 0.1 copy.6
  3.6 0.0 copy-start
  3.6 2.1 %copy-done = bf16[20,1,2,3,128,128]{5,4,3,2,1,0:T(8,128)(2,1)S(1)} copy-done((bf16[20,1,2,3,128,128]{5,4,3,2,1,0:T(8,128)(2,1)S(1)}, bf16[20,1,2,3,128,128]{5,4,3,2,1,0:T(8,128)(2,1)}, u32[]{:S(2)}) %copy-start) | copy-done | bytes 3932184
  5.7 66.4 %galerkin.1 = bf16[32,16,128]{2,1,0:T(8,128)(2,1)S(1)} custom-call(s32[2,3]{1,0:T(2,128)S(1)} %add_bitcast_fusion.cols, bf16[33,16,128]{2,1,0:T(8,128)(2,1)S(1)} %bitcast.19, bf16[80,256]{1,0:T(8,128)(2,1)S(1)} %reshape.36.chunk, bf16[20,2,3,128,128]{4,3,2,1,0:T(8,128)(2,1)S(1)} %bitcast.21), custom_call_target="tpu_custom_call" | custom-call | flops 2000000000 | bytes 8000000 | tf_op jit(solution)/shard_map/galerkin/pallas_call | solution.py:326
  72.1 0.1 copy.8
  72.2 0.7 reshape.39
  (2 shorter events, 0.0 us)
Async XLA Ops:
  3.6 2.1 %copy-start = (bf16[20,1,2,3,128,128]{5,4,3,2,1,0:T(8,128)(2,1)S(1)}, bf16[20,1,2,3,128,128]{5,4,3,2,1,0:T(8,128)(2,1)}, u32[]{:S(2)}) copy-start(bf16[20,1,2,3,128,128]{5,4,3,2,1,0:T(8,128)(2,1)} %param.6) | copy-start | bytes 11796484

commit v2 on v1

--- a/solution.py
+++ b/solution.py
@@ -2,6 +2,7 @@
 import jax.numpy as jnp
 from jax import lax
 from jax.experimental import pallas as pl
+from jax.experimental.layout import Layout, with_layout_constraint
 from jax.experimental.pallas import tpu as pltpu
 from jax.sharding import PartitionSpec as P
 
@@ -29,8 +30,8 @@
     return lax.dot_general(a, b, (((1,), (1,)), ((), ())), preferred_element_type=F32)
 
 
-def kernel(cols, u, chunk, tiles, out,
-           tv, uin, ufix, vbuf, xraw, xw, eraw, ew, zbuf, acc, ob, oin, fb,
+def kernel(colidx, cells, coupling, pattern, tiles, out,
+           u, chunk, tv, uin, ufix, vbuf, xraw, xw, eraw, ew, zbuf, acc, ob, oin, fb,
            s_t, s_v, r_v, s_e, r_e, s_u, r_u, s_a, r_a, s_b, r_b, s_d, r_d, s_x, r_x, s_o, r_o, s_p, r_p):
     rank = lax.axis_index("chaos")
     s = lax.axis_index("space")
@@ -56,6 +57,7 @@
     mate = (yx * 2 + h) * 2 + 1 - c
     low, high = s > 0, s < 7
     flat = yx * 4 + c
+    first_col = s * 128 + (rank // 2) * 4 - 2
 
     load = pltpu.make_async_copy(tiles, tv, s_t)
     load.start()
@@ -91,6 +93,24 @@
 
     lax.fori_loop(1, 32, greet_plane, 0)
     has_halo = (low & (h == 0)) | (high & (h == 1))
+
+    row = lax.broadcasted_iota(jnp.int32, (80, M), 0)
+    term = lax.broadcasted_iota(jnp.int32, (80, M), 1)
+    spread = jnp.where(row // 4 == term, 1.0, 0.0).astype(BF)
+    block = lax.broadcasted_iota(jnp.int32, (4, 256), 0)
+    column = lax.broadcasted_iota(jnp.int32, (4, 256), 1)
+    widen = jnp.where(column // CBLK == block, 1.0, 0.0).astype(BF)
+    mask = matmul(matmul_nt(spread, pattern[y].astype(F32).astype(BF)).astype(BF), widen)
+    out_row = lax.broadcasted_iota(jnp.int32, (80, 160), 0)
+    in_row = lax.broadcasted_iota(jnp.int32, (80, 160), 1)
+    raw = coupling[...].reshape(160, TILE)
+    for part in range(2):
+        take = jnp.where(in_row == (out_row // 4) * 8 + part * 4 + out_row % 4, 1.0, 0.0).astype(BF)
+        lanes = slice(part * TILE, part * TILE + TILE)
+        chunk[:, lanes] = (matmul(take, raw) * mask[:, lanes]).astype(BF)
+
+    gap = jnp.zeros((8, TILE), BF)
+    u[...] = jnp.concatenate([gap, cells[...].reshape(512, TILE), gap], axis=0).reshape(UNITS, 16, TILE)
     pl.semaphore_wait(barrier, 32 + low.astype(jnp.int32) + high.astype(jnp.int32) + has_halo.astype(jnp.int32))
 
     send_right = remote(u.at[UNITS - 1], vbuf.at[h], s_v.at[0], r_v.at[h], flat, jnp.minimum(s + 1, 7))
@@ -239,7 +259,7 @@
 
     def stage_one(half):
         for r in range(2):
-            picked = [xw[half, cols[r, q]] for q in range(3)]
+            picked = [xw[half, jnp.clip(colidx[0, r, q] - first_col, 0, 7)] for q in range(3)]
             pair = jnp.concatenate(picked[:2], axis=1)
 
             def some(kg, carry):
@@ -270,28 +290,35 @@
     stage_one(1)
     total = (acc[...] + stage_two(1)).astype(BF)
 
-    o_perm = perm(256, lambda o: ((o % 64) // 4) * 16 + (o // 128) * 8 + ((o % 128) // 64) * 4 + o % 4)
+    o_perm = perm(256, lambda o: ((o % 64) // 4) * 16 + ((o % 128) // 64) * 8 + (o // 128) * 4 + o % 4)
     ob[...] = matmul_nt(o_perm, total).astype(BF)
-    cross_o = remote(ob.at[pl.ds(pl.multiple_of((1 - h) * 128, 128), 128)], oin, s_o, r_o, anti)
-    cross_o.start()
-    mine = ob[pl.ds(pl.multiple_of(h * 128, 128), 128)]
+    swap = remote(ob.at[pl.ds(pl.multiple_of((1 - c) * 128, 128), 128)], oin, s_o, r_o, mate)
+    swap.start()
+    mine = ob[pl.ds(pl.multiple_of(c * 128, 128), 128)]
     f_perm = perm(256, lambda o: ((o % 16) // 4) * 64 + (o // 16) * 4 + o % 4)
-    cross_o.wait_recv()
+    swap.wait_recv()
     theirs = oin[...]
-    lower = jnp.where(h == 0, mine, theirs)
-    upper = jnp.where(h == 0, theirs, mine)
-    for dest_c in range(2):
-        rows = slice(dest_c * 64, dest_c * 64 + 64)
+    lower = jnp.where(c == 0, mine, theirs)
+    upper = jnp.where(c == 0, theirs, mine)
+    for dest_h in range(2):
+        rows = slice(dest_h * 64, dest_h * 64 + 64)
         stack = jnp.concatenate([lower[rows, :TILE], lower[rows, TILE:], upper[rows, :TILE], upper[rows, TILE:]], axis=0)
-        fb[dest_c] = matmul(f_perm, stack).astype(BF).reshape(16, 16, TILE)
-
-    def give(d, carry):
-        other = (slot + d) % 32
-        remote(fb.at[other % 2, other // 2], out.at[slot], s_p, r_p, in_plane(other // 2, other % 2)).start()
+        fb[dest_h] = matmul(f_perm, stack).astype(BF).reshape(16, 16, TILE)
+    chip = yx * 2 + h
+
+    def give_far(d, carry):
+        other = (yx + d) % 16
+        remote(fb.at[1 - h, other], out.at[chip], s_p, r_p, (other * 2 + 1 - h) * 2 + c).start()
         return carry
 
-    lax.fori_loop(1, 32, give, 0)
-    out[slot] = fb[c, yx]
+    def give_near(d, carry):
+        other = (yx + d) % 16
+        remote(fb.at[h, other], out.at[chip], s_p, r_p, (other * 2 + h) * 2 + c).start()
+        return carry
+
+    lax.fori_loop(0, 16, give_far, 0)
+    lax.fori_loop(1, 16, give_near, 0)
+    out[chip] = fb[h, yx]
 
     @pl.when(high)
     def _():
@@ -307,29 +334,28 @@
     for half in (0, 1):
         finish_e(half)
         wait_for(xraw.at[half, pl.ds(0, 31)], s_x.at[half])
-    cross_o.wait_send()
+    swap.wait_send()
     wait_for(out.at[pl.ds(0, 31)], s_p)
     wait_for(out.at[pl.ds(0, 31)], r_p)
 
 
 def shards(panels, tiles, coupling, pattern, colidx):
-    rank = lax.axis_index("chaos")
-    space = lax.axis_index("space")
-    cells = jnp.transpose(panels.reshape(4, 128, TILE), (1, 0, 2)).reshape(512, TILE)
-    units = jnp.pad(cells, ((8, 8), (0, 0))).reshape(UNITS, 16, TILE)
-    own_pattern = lax.dynamic_index_in_dim(pattern, rank // 16, 1, keepdims=False).astype(BF)
-    mask = jnp.broadcast_to(own_pattern[:, None, :, None], (M, 4, 4, CBLK)).reshape(M, 4, 256)
-    chunk = (jnp.transpose(coupling, (1, 0, 2)) * mask).reshape(80, 256)
-    cols = colidx[0] - (space * 128 + (rank // 2) * 4) + 2
+    cells = with_layout_constraint(panels.reshape(4, 128, TILE), Layout((1, 0, 2)))
+    cells = jnp.transpose(cells, (1, 0, 2)).reshape(32, 16, TILE)
+    values = with_layout_constraint(coupling.reshape(4, M, 2, TILE), Layout((1, 2, 0, 3)))
+    values = jnp.transpose(values, (1, 2, 0, 3)).reshape(10, 16, TILE)
+    blocks = jnp.transpose(pattern, (1, 2, 0))
     vmem = pl.BlockSpec(memory_space=pltpu.VMEM)
     dma = pltpu.SemaphoreType.DMA
     result = pl.pallas_call(
         kernel,
         name="galerkin",
         out_shape=jax.ShapeDtypeStruct((32, 16, TILE), BF),
-        in_specs=[pl.BlockSpec(memory_space=pltpu.SMEM), vmem, vmem, pl.BlockSpec(memory_space=pl.ANY)],
+        in_specs=[pl.BlockSpec(memory_space=pltpu.SMEM), vmem, vmem, vmem, pl.BlockSpec(memory_space=pl.ANY)],
         out_specs=vmem,
         scratch_shapes=[
+            pltpu.VMEM((UNITS, 16, TILE), BF),
+            pltpu.VMEM((80, 256), BF),
             pltpu.VMEM((M, 2, 3, TILE, TILE), BF),
             pltpu.VMEM((UNITS, 16, TILE), BF),
             pltpu.VMEM((2, 2, 16, TILE), BF),
@@ -347,11 +373,11 @@
             dma((2, 2)), dma((2, 2)), dma((2, 2)), dma((2, 2)), dma((2,)), dma((2,)), dma((2,)), dma((2,)),
             dma, dma, dma, dma,
         ],
-        compiler_params=pltpu.CompilerParams(collective_id=0, has_side_effects=True, vmem_limit_bytes=40 << 20),
+        compiler_params=pltpu.CompilerParams(collective_id=0, has_side_effects=True, vmem_limit_bytes=62 << 20),
         cost_estimate=pl.CostEstimate(flops=2_000_000_000, bytes_accessed=8_000_000, transcendentals=0),
-    )(cols, units, chunk, tiles.reshape(M, 2, 3, TILE, TILE))
-    parts = result.reshape(16, 2, 2, 2, 4, TILE)
-    return jnp.transpose(parts, (4, 0, 2, 1, 3, 5)).reshape(4, 128 * TILE)
+    )(colidx, cells, values, blocks, tiles.reshape(M, 2, 3, TILE, TILE))
+    result = jnp.transpose(result.reshape(128, 4, TILE), (1, 0, 2))
+    return with_layout_constraint(result, Layout((1, 0, 2))).reshape(4, 128 * TILE)
 
 
 def solution(mesh):

time: 73.9 us -> 67.5 us (0.913)
  local copies, waits for them, and re-layouts: 4.26 us -> 1.61 us
  other arithmetic: 2.18 us -> 0 us
  Pallas kernels: 66.4 us -> 64.8 us
    pallas_call x1, Pallas kernels: 66.4 us -> 64.8 us  [shards(): pl.pallas_call(kernel, name='galerkin', out_shape=jax.ShapeDtypeStruct((3...]
    unnamed x3 -> x1, local copies, waits for them, and re-layouts: 3.03 us -> 1.61 us
    mul x1 -> x0, other arithmetic: 0.81 us -> none  [shards(): chunk = (jnp.transpose(coupling, (1, 0, 2)) * mask).reshape(80, 256)]
where the time goes in v2:
time: 67.5 us; the launch traced here: 66.5 us
  Pallas kernels  64.8 us (96%)
  local copies, waits for them, and re-layouts  1.61 us (2%)
    pallas_call x1, Pallas kernels, shards(): pl.pallas_call(kernel, name='galerkin', out_shape=jax.ShapeDtypeStruct((3...  64.8 us
    unnamed x1, local copies, waits for them, and re-layouts  1.61 us

profile of v2, /device:TPU:1, one launch (start us, length us, event | category | flops | bytes accessed | tf_op | source)
XLA Modules:
  0.0 66.5 jit_solution(15244266568604648795)
XLA Ops:
  0.0 64.8 %galerkin.1 = bf16[32,16,128]{2,1,0:T(8,128)(2,1)} custom-call(s32[1,2,3]{2,1,0:T(2,128)} %colidx.1, bf16[32,16,128]{2,1,0:T(8,128)(2,1)} %bitcast.19, bf16[10,16,128]{2,1,0:T(8,128)(2,1)} %bitcast.20, s32[4,4,20]{2,1,0:T(4,128)} %bitcast.21, bf16[20,2,3,128,128]{4,3,2,1,0:T(8,128)(2,1)} %bitcast.18), custom_call_target="tpu_custom_call" | custom-call | flops 2000000000 | bytes 8000000 | tf_op jit(solution)/shard_map/galerkin/pallas_call | solution.py:350
  64.9 1.6 %copy.7 = bf16[4,16384]{1,0:T(4,128)(2,1)} copy(bf16[4,16384]{1,0:T(4,128)(2,1)} %bitcast.17) | data formatting | bytes 262144

commit v3 on v2

--- a/solution.py
+++ b/solution.py
@@ -30,9 +30,9 @@
     return lax.dot_general(a, b, (((1,), (1,)), ((), ())), preferred_element_type=F32)
 
 
-def kernel(colidx, cells, coupling, pattern, tiles, out,
-           u, chunk, tv, uin, ufix, vbuf, xraw, xw, eraw, ew, zbuf, acc, ob, oin, fb,
-           s_t, s_v, r_v, s_e, r_e, s_u, r_u, s_a, r_a, s_b, r_b, s_d, r_d, s_x, r_x, s_o, r_o, s_p, r_p):
+def kernel(colidx, cells_in, coupling_in, pattern_in, tiles, out,
+           cells, coupling, pattern, ends, u, chunk, tv, uin, vbuf, xraw, xw, eraw, ew, zbuf, acc, ob, oin, fb,
+           s_c, s_t, s_v, r_v, s_e, r_e, s_u, r_u, s_a, r_a, s_b, r_b, s_d, r_d, s_x, r_x, s_o, r_o, s_p, r_p):
     rank = lax.axis_index("chaos")
     s = lax.axis_index("space")
     c = rank % 2
@@ -56,11 +56,13 @@
     anti = (yx * 2 + 1 - h) * 2 + c
     mate = (yx * 2 + h) * 2 + 1 - c
     low, high = s > 0, s < 7
+    place = jnp.where(s < 4, s, 7 - s)
+    at_border = place == 0
+    border = jnp.where(s < 4, 7, 0)
+    beyond = [jnp.where(s == 0, 7 - j, j) for j in range(4)]
+    peers = [(s // 4) * 4 + (s + d) % 4 for d in (1, 2, 3)]
     flat = yx * 4 + c
     first_col = s * 128 + (rank // 2) * 4 - 2
-
-    load = pltpu.make_async_copy(tiles, tv, s_t)
-    load.start()
 
     barrier = pltpu.get_barrier_semaphore()
 
@@ -69,6 +71,18 @@
                             device_id_type=pl.DeviceIdType.MESH)
 
     greet(anti, s)
+
+    @pl.when(at_border)
+    def _():
+        for j in range(4):
+            greet(anti, beyond[j])
+
+    @pl.when(jnp.logical_not(at_border))
+    def _():
+        greet(anti, border)
+
+    for peer in peers:
+        greet(rank, peer)
 
     @pl.when(high)
     def _():
@@ -91,8 +105,15 @@
         greet(in_plane(other // 2, other % 2), s)
         return carry
 
-    lax.fori_loop(1, 32, greet_plane, 0)
+    lax.fori_loop(1, 32, greet_plane, 0, unroll=True)
     has_halo = (low & (h == 0)) | (high & (h == 1))
+
+    fetches = []
+    for i, (src, dst) in enumerate(((coupling_in, coupling), (pattern_in, pattern), (cells_in, cells))):
+        fetches.append(pltpu.make_async_copy(src, dst, s_c.at[i]))
+        fetches[-1].start()
+    load = pltpu.make_async_copy(tiles, tv, s_t)
+    load.start()
 
     row = lax.broadcasted_iota(jnp.int32, (80, M), 0)
     term = lax.broadcasted_iota(jnp.int32, (80, M), 1)
@@ -100,6 +121,8 @@
     block = lax.broadcasted_iota(jnp.int32, (4, 256), 0)
     column = lax.broadcasted_iota(jnp.int32, (4, 256), 1)
     widen = jnp.where(column // CBLK == block, 1.0, 0.0).astype(BF)
+    fetches[0].wait()
+    fetches[1].wait()
     mask = matmul(matmul_nt(spread, pattern[y].astype(F32).astype(BF)).astype(BF), widen)
     out_row = lax.broadcasted_iota(jnp.int32, (80, 160), 0)
     in_row = lax.broadcasted_iota(jnp.int32, (80, 160), 1)
@@ -109,12 +132,15 @@
         lanes = slice(part * TILE, part * TILE + TILE)
         chunk[:, lanes] = (matmul(take, raw) * mask[:, lanes]).astype(BF)
 
+    fetches[2].wait()
     gap = jnp.zeros((8, TILE), BF)
     u[...] = jnp.concatenate([gap, cells[...].reshape(512, TILE), gap], axis=0).reshape(UNITS, 16, TILE)
-    pl.semaphore_wait(barrier, 32 + low.astype(jnp.int32) + high.astype(jnp.int32) + has_halo.astype(jnp.int32))
-
-    send_right = remote(u.at[UNITS - 1], vbuf.at[h], s_v.at[0], r_v.at[h], flat, jnp.minimum(s + 1, 7))
-    send_left = remote(u.at[0], vbuf.at[1 - h], s_v.at[1], r_v.at[1 - h], flat + 2, jnp.maximum(s - 1, 0))
+    ends[0] = u[0]
+    ends[1] = u[UNITS - 1]
+    pl.semaphore_wait(barrier, jnp.where(at_border, 39, 36) + low.astype(jnp.int32) + high.astype(jnp.int32) + has_halo.astype(jnp.int32))
+
+    send_right = remote(ends.at[1], vbuf.at[h], s_v.at[0], r_v.at[h], flat, jnp.minimum(s + 1, 7))
+    send_left = remote(ends.at[0], vbuf.at[1 - h], s_v.at[1], r_v.at[1 - h], flat + 2, jnp.maximum(s - 1, 0))
 
     @pl.when(high)
     def _():
@@ -124,14 +150,46 @@
     def _():
         send_left.start()
 
-    cross_e = remote(chunk, eraw.at[c, 1, y, x], s_e, r_e, anti)
-    cross_e.start()
     crossings = []
     for i, shift in enumerate(ORDER):
         start = ((y + shift) % 4) * 8 + 1 - h
         crossing = remote(u.at[pl.ds(start, 8)], uin.at[pl.ds(start, 8)], s_u.at[i], r_u.at[i], anti)
-        crossing.start()
         crossings.append(crossing)
+
+    theirs_e = eraw.at[c, 1, y, x]
+
+    def unit(j):
+        return pl.ds(pl.multiple_of(j * 16, 16), 16)
+
+    @pl.when(at_border)
+    def _():
+        for j in range(5):
+            remote(chunk.at[unit(j)], theirs_e.at[unit(j)], s_e.at[0], r_e.at[0], anti, beyond[j % 4]).start()
+
+    def exchange_e():
+        def share(j):
+            for peer in peers:
+                remote(theirs_e.at[unit(j)], theirs_e.at[unit(j)], s_e.at[1], r_e.at[1], rank, peer).start()
+
+        @pl.when(at_border)
+        def _():
+            wait_for(theirs_e.at[pl.ds(0, 32)], r_e.at[0])
+            share(4)
+
+        @pl.when(jnp.logical_not(at_border))
+        def _():
+            wait_for(theirs_e.at[pl.ds(0, 16)], r_e.at[0])
+
+        share(place)
+
+    def exchanged_e():
+        @pl.when(at_border)
+        def _():
+            wait_for(theirs_e.at[pl.ds(0, 48)], r_e.at[1])
+
+        @pl.when(jnp.logical_not(at_border))
+        def _():
+            wait_for(theirs_e.at[pl.ds(0, 64)], r_e.at[1])
 
     first = pl.ds(0, SPLIT)
     second = pl.ds(SPLIT, 80 - SPLIT)
@@ -169,69 +227,28 @@
         wait_for(part.at[pl.ds(0, 3), :, second], s_b.at[half, 1])
         wait_for(part, s_d.at[half])
 
+    crossings[0].start()
     phase_a(chunk, 0)
     eraw[c, 0, y, x] = chunk[...]
 
-    hub = 15 * h
     slot = yx * 2 + c
 
-    def serve_row(src, half, shift):
-        dest_y = (y + shift) % 4
-
-        def serve(i, carry):
-            dest = dest_y * 4 + (x + i // 2) % 4
-            dest_c = (c + i % 2) % 2
-
-            @pl.when((dest != hub) & (dest * 2 + dest_c != slot))
-            def _():
+    def serve_row(src, half, dest_y, skip_own):
+        for dx in range(4):
+            for dc in range(2):
+                if skip_own and dx == 0 and dc == 0:
+                    continue
+                dest = dest_y * 4 + (x + dx) % 4
                 remote(src.at[pl.ds(dest * 2 + h, 2)], xraw.at[half, slot], s_x.at[half], r_x.at[half],
-                       in_plane(dest, dest_c)).start()
-
-            return carry
-
-        lax.fori_loop(0, 8, serve, 0)
-
-    def serve_hub(src, half):
+                       in_plane(dest, (c + dc) % 2)).start()
+        if skip_own:
+            xraw[half, slot] = src[pl.ds(yx * 2 + h, 2)]
+
+    def merge_halo(src, half):
         @pl.when(has_halo)
         def _():
             wait_for(vbuf.at[half], r_v.at[half])
-
-        @pl.when(jnp.logical_not(has_halo))
-        def _():
-            vbuf[half] = jnp.zeros((16, TILE), BF)
-
-        halo = vbuf[half]
-        none = jnp.zeros_like(halo)
-        ufix[half, 0] = src[31 * h] + jnp.where(h == 0, halo, none)
-        ufix[half, 1] = src[31 * h + 1] + jnp.where(h == 1, halo, none)
-        for dest_c in (0, 1):
-            @pl.when(hub * 2 + dest_c != slot)
-            def _():
-                remote(ufix.at[half], xraw.at[half, slot], s_x.at[half], r_x.at[half],
-                       in_plane(hub, dest_c)).start()
-
-        @pl.when(yx == hub)
-        def _():
-            xraw[half, slot] = ufix[half]
-
-        @pl.when(yx != hub)
-        def _():
-            xraw[half, slot] = src[pl.ds(yx * 2 + h, 2)]
-
-    for shift in ORDER:
-        serve_row(u, 0, shift)
-    phase_b(0)
-    serve_hub(u, 0)
-
-    cross_e.wait_recv()
-    phase_a(eraw.at[c, 1, y, x], 1)
-    phase_d(0)
-    for i, shift in enumerate(ORDER):
-        crossings[i].wait_recv()
-        serve_row(uin, 1, shift)
-        if i == 1:
-            phase_b(1)
-    serve_hub(uin, 1)
+            src[32 * h] = src[32 * h] + vbuf[half]
 
     x_perm = perm(256, lambda o: ((o % 32) // 4) * 32 + (o // 32) * 4 + o % 4)
     e_perm = perm(256, lambda o: ((o % 8) // 4) * 128 + ((o % 64) // 8) * 16 + (o // 64) * 4 + o % 4)
@@ -255,7 +272,7 @@
                     ew[half, kg * 4 + k, pl.ds(g * 64, 64)] = part[k * 64:(k + 1) * 64]
             return carry
 
-        lax.fori_loop(0, 5, group, 0)
+        lax.fori_loop(0, 5, group, 0, unroll=True)
 
     def stage_one(half):
         for r in range(2):
@@ -271,20 +288,45 @@
                     zbuf[kg * 2 + k // 2, pl.ds(r * TILE, TILE), pl.ds((k % 2) * TILE, TILE)] = z[k * TILE:(k + 1) * TILE]
                 return carry
 
-            lax.fori_loop(0, 5, some, 0)
+            lax.fori_loop(0, 5, some, 0, unroll=True)
 
     def stage_two(half):
         def pair_of(kk, total):
             return total + matmul(zbuf[kk], ew[half, pl.ds(kk * 2, 2)].reshape(256, 256))
 
-        return lax.fori_loop(0, 10, pair_of, jnp.zeros((256, 256), F32))
-
-    load.wait()
-    ready_x(0)
-    stage_one(0)
-    phase_d(1)
-    ready_e(0)
-    acc[...] = stage_two(0)
+        return lax.fori_loop(0, 10, pair_of, jnp.zeros((256, 256), F32), unroll=True)
+
+    merge_halo(u, 0)
+    exchange_e()
+    for crossing in crossings[1:]:
+        crossing.start()
+    for shift in ORDER[:2]:
+        serve_row(u, 0, (y + shift) % 4, shift == 0)
+    phase_b(0)
+    exchanged_e()
+    phase_a(eraw.at[c, 1, y, x], 1)
+    for shift in ORDER[2:]:
+        serve_row(u, 0, (y + shift) % 4, shift == 0)
+    phase_d(0)
+    phase_b(1)
+    for i, shift in enumerate(ORDER):
+        dest_y = (y + shift) % 4
+        crossings[i].wait_recv()
+
+        @pl.when(dest_y == 3 * h)
+        def _():
+            merge_halo(uin, 1)
+
+        serve_row(uin, 1, dest_y, shift == 0)
+        if i == 0:
+            load.wait()
+            ready_x(0)
+            ready_e(0)
+        if i == 1:
+            stage_one(0)
+            phase_d(1)
+        if i == 2:
+            acc[...] = stage_two(0)
     ready_e(1)
     ready_x(1)
     stage_one(1)
@@ -316,8 +358,8 @@
         remote(fb.at[h, other], out.at[chip], s_p, r_p, (other * 2 + h) * 2 + c).start()
         return carry
 
-    lax.fori_loop(0, 16, give_far, 0)
-    lax.fori_loop(1, 16, give_near, 0)
+    lax.fori_loop(0, 16, give_far, 0, unroll=True)
+    lax.fori_loop(1, 16, give_near, 0, unroll=True)
     out[chip] = fb[h, yx]
 
     @pl.when(high)
@@ -328,7 +370,13 @@
     def _():
         send_left.wait_send()
 
-    cross_e.wait_send()
+
+    @pl.when(at_border)
+    def _():
+        wait_for(chunk, s_e.at[0])
+        wait_for(theirs_e.at[pl.ds(0, 48)], s_e.at[1])
+
+    wait_for(theirs_e.at[pl.ds(0, 48)], s_e.at[1])
     for crossing in crossings:
         crossing.wait_send()
     for half in (0, 1):
@@ -351,14 +399,17 @@
         kernel,
         name="galerkin",
         out_shape=jax.ShapeDtypeStruct((32, 16, TILE), BF),
-        in_specs=[pl.BlockSpec(memory_space=pltpu.SMEM), vmem, vmem, vmem, pl.BlockSpec(memory_space=pl.ANY)],
+        in_specs=[pl.BlockSpec(memory_space=pltpu.SMEM)] + [pl.BlockSpec(memory_space=pltpu.HBM)] * 4,
         out_specs=vmem,
         scratch_shapes=[
+            pltpu.VMEM((32, 16, TILE), BF),
+            pltpu.VMEM((10, 16, TILE), BF),
+            pltpu.VMEM((4, 4, M), jnp.int32),
+            pltpu.VMEM((2, 16, TILE), BF),
             pltpu.VMEM((UNITS, 16, TILE), BF),
             pltpu.VMEM((80, 256), BF),
             pltpu.VMEM((M, 2, 3, TILE, TILE), BF),
             pltpu.VMEM((UNITS, 16, TILE), BF),
-            pltpu.VMEM((2, 2, 16, TILE), BF),
             pltpu.VMEM((2, 16, TILE), BF),
             pltpu.VMEM((2, 32, 2, 16, TILE), BF),
             pltpu.VMEM((2, 8, TILE, TILE), BF),
@@ -369,11 +420,11 @@
             pltpu.VMEM((256, 256), BF),
             pltpu.VMEM((TILE, 256), BF),
             pltpu.VMEM((2, 16, 16, TILE), BF),
-            dma, dma((2,)), dma((2,)), dma, dma, dma((4,)), dma((4,)),
+            dma((3,)), dma, dma((2,)), dma((2,)), dma((2,)), dma((2,)), dma((4,)), dma((4,)),
             dma((2, 2)), dma((2, 2)), dma((2, 2)), dma((2, 2)), dma((2,)), dma((2,)), dma((2,)), dma((2,)),
             dma, dma, dma, dma,
         ],
-        compiler_params=pltpu.CompilerParams(collective_id=0, has_side_effects=True, vmem_limit_bytes=62 << 20),
+        compiler_params=pltpu.CompilerParams(collective_id=0, has_side_effects=True, vmem_limit_bytes=56 << 20),
         cost_estimate=pl.CostEstimate(flops=2_000_000_000, bytes_accessed=8_000_000, transcendentals=0),
     )(colidx, cells, values, blocks, tiles.reshape(M, 2, 3, TILE, TILE))
     result = jnp.transpose(result.reshape(128, 4, TILE), (1, 0, 2))

time: 67.5 us -> 60 us (0.89)
  the two profiles are of different devices: /device:TPU:1 before, /device:TPU:128 now
where the time goes in v3:
time: 60 us; the launch traced here: 59.9 us
  Pallas kernels  58.3 us (97%)
  local copies, waits for them, and re-layouts  1.61 us (3%)
    pallas_call x1, Pallas kernels, shards(): pl.pallas_call(kernel, name='galerkin', out_shape=jax.ShapeDtypeStruct((3...  58.3 us
    unnamed x1, local copies, waits for them, and re-layouts  1.61 us

profile of v3, /device:TPU:128, one launch (start us, length us, event | category | flops | bytes accessed | tf_op | source)
XLA Modules:
  0.0 59.9 jit_solution(1139894664124645422)
XLA Ops:
  0.0 58.3 %galerkin.1 = bf16[32,16,128]{2,1,0:T(8,128)(2,1)} custom-call(s32[1,2,3]{2,1,0:T(2,128)} %colidx.1, bf16[32,16,128]{2,1,0:T(8,128)(2,1)} %bitcast.19, bf16[10,16,128]{2,1,0:T(8,128)(2,1)} %bitcast.20, s32[4,4,20]{2,1,0:T(4,128)} %bitcast.21, bf16[20,2,3,128,128]{4,3,2,1,0:T(8,128)(2,1)} %bitcast.18), custom_call_target="tpu_custom_call" | custom-call | flops 2000000000 | bytes 8000000 | tf_op jit(solution)/shard_map/galerkin/pallas_call | solution.py:398
  58.3 1.6 %copy.7 = bf16[4,16384]{1,0:T(4,128)(2,1)} copy(bf16[4,16384]{1,0:T(4,128)(2,1)} %bitcast.17) | data formatting | bytes 262144

commit v4 on v3

--- a/solution.py
+++ b/solution.py
@@ -307,8 +307,6 @@
     phase_a(eraw.at[c, 1, y, x], 1)
     for shift in ORDER[2:]:
         serve_row(u, 0, (y + shift) % 4, shift == 0)
-    phase_d(0)
-    phase_b(1)
     for i, shift in enumerate(ORDER):
         dest_y = (y + shift) % 4
         crossings[i].wait_recv()
@@ -319,17 +317,19 @@
 
         serve_row(uin, 1, dest_y, shift == 0)
         if i == 0:
+            phase_d(0)
+            phase_b(1)
             load.wait()
             ready_x(0)
-            ready_e(0)
         if i == 1:
             stage_one(0)
-            phase_d(1)
+            ready_e(0)
         if i == 2:
             acc[...] = stage_two(0)
-    ready_e(1)
+    phase_d(1)
     ready_x(1)
     stage_one(1)
+    ready_e(1)
     total = (acc[...] + stage_two(1)).astype(BF)
 
     o_perm = perm(256, lambda o: ((o % 64) // 4) * 16 + ((o % 128) // 64) * 8 + (o // 128) * 4 + o % 4)

time: 60 us -> 57.6 us (0.960)
  Pallas kernels: 58.3 us -> 55.8 us
    pallas_call x1, Pallas kernels: 58.3 us -> 55.8 us  [shards(): pl.pallas_call(kernel, name='galerkin', out_shape=jax.ShapeDtypeStruct((3...]
where the time goes in v4:
time: 57.6 us; the launch traced here: 57.4 us
  Pallas kernels  55.8 us (97%)
  local copies, waits for them, and re-layouts  1.61 us (3%)
    pallas_call x1, Pallas kernels, shards(): pl.pallas_call(kernel, name='galerkin', out_shape=jax.ShapeDtypeStruct((3...  55.8 us
    unnamed x1, local copies, waits for them, and re-layouts  1.61 us

profile of v4, /device:TPU:128, one launch (start us, length us, event | category | flops | bytes accessed | tf_op | source)
XLA Modules:
  0.0 57.4 jit_solution(7036341557638054827)
XLA Ops:
  0.0 55.8 %galerkin.1 = bf16[32,16,128]{2,1,0:T(8,128)(2,1)} custom-call(s32[1,2,3]{2,1,0:T(2,128)} %colidx.1, bf16[32,16,128]{2,1,0:T(8,128)(2,1)} %bitcast.19, bf16[10,16,128]{2,1,0:T(8,128)(2,1)} %bitcast.20, s32[4,4,20]{2,1,0:T(4,128)} %bitcast.21, bf16[20,2,3,128,128]{4,3,2,1,0:T(8,128)(2,1)} %bitcast.18), custom_call_target="tpu_custom_call" | custom-call | flops 2000000000 | bytes 8000000 | tf_op jit(solution)/shard_map/galerkin/pallas_call | solution.py:398
  55.8 1.6 %copy.7 = bf16[4,16384]{1,0:T(4,128)(2,1)} copy(bf16[4,16384]{1,0:T(4,128)(2,1)} %bitcast.17) | data formatting | bytes 262144
